TPU v7x, 256 devices: a whole 4x4x8 slice. The times are simulated.
256 devices in a mesh: rep: 4 (over z_lo, core), ep: 64 (over y, x, z_hi).
Axes of the slice: x: 4, y: 4, z: 8 (z_hi: 4, z_lo: 2; z = z_hi * 2 + z_lo), core: 2. Of those that a mesh axis runs over, the one named last changes fastest.
Arguments:
- deltas: bfloat16 [4, 64, 2048, 768], P('rep', None, 'ep'), may hold values from -3 to 3
- master: float32 [64, 64, 4, 8, 768], P(None, 'ep', 'rep'), may hold values from -6 to 6
- momentum: float32 [64, 64, 4, 8, 768], P(None, 'ep', 'rep'), may hold values from -3 to 3
- hidden: bfloat16 [4, 8192, 2048], P(None, ('rep', 'ep')), may hold values from -6 to 6
- expert_ids: int32 [4, 8192, 8], P(None, ('rep', 'ep')), may hold values from 0 to 63, as said below
- gate_weights: float32 [4, 8192, 8], P(None, ('rep', 'ep')), may hold values from 0.1 to 0.4
Outputs:
- engine_weights: bfloat16 [64, 2048, 768], P('ep')
- momentum_out: float32 [64, 64, 4, 8, 768], P(None, 'ep', 'rep')
- decoded: bfloat16 [4, 8192, 768], P(None, ('rep', 'ep'))
Inputs may be any that keep to these rules, and one draw needn't show every extreme that they name: `expert_ids`: in every step, each row names 8 different experts; among the 32 rows of one device no expert is named by more than 6 rows, and on every device in every step some expert is named by exactly 6 rows.
All inputs are finite; a program needn't handle non-finite values.
Results may differ from a plain program's by a relative error of at most 0.013.
Values may be sent and summed in bfloat16 or wider, within the bound.
No kernel may reach another device: no remote copies, remote signals or barrier semaphores. Data moves between devices by JAX's collectives and lax.ppermute only.
A program may use at most 128 MiB of HBM per device.

v0:
```python
import math

import jax
import jax.numpy as jnp
from jax import lax
from jax.sharding import PartitionSpec as P

CAP = 6


outer_momentum = 0.9
outer_rate = 0.7


def routing_tables(route_ids, route_gates, experts, slots):
    row_count, fanout = route_ids.shape
    flat_ids = route_ids.reshape(row_count * fanout)
    onehot = (flat_ids[:, None] == jnp.arange(experts, dtype=jnp.int32)[None, :]).astype(jnp.int32)
    before = jnp.cumsum(onehot, axis=0) - onehot
    position = jnp.sum(before * onehot, axis=1)
    target = flat_ids * slots + position
    placed = (target[:, None] == jnp.arange(experts * slots, dtype=jnp.int32)[None, :]).reshape(
        row_count, fanout, experts * slots
    )
    sending = jnp.any(placed, axis=1).T.astype(jnp.bfloat16)
    weights = jnp.sum(jnp.where(placed, route_gates[:, :, None], jnp.float32(0.0)), axis=1)
    return (sending, weights)


def weigh_back(weights, returned):
    summed = jnp.dot(weights, returned.astype(jnp.float32), precision=lax.Precision.HIGHEST)
    return summed.astype(jnp.bfloat16)


def local(deltas, master, momentum, hidden, expert_ids, gate_weights):
    experts = deltas.shape[1]
    hidden_width = deltas.shape[3]
    replicas = lax.axis_size("rep")
    owners = lax.axis_size("ep")
    owned_count = experts // owners
    sub_rows = master.shape[3]
    model_width = deltas.shape[2] * owners
    summed = lax.psum_scatter(
        deltas[0].astype(jnp.float32).astype(jnp.bfloat16), "rep", scatter_dimension=1, tiled=True
    ).astype(jnp.float32)
    params = master.reshape(experts, sub_rows, hidden_width)
    velocity_old = momentum.reshape(experts, sub_rows, hidden_width)
    outer_grad = summed / replicas
    velocity = outer_momentum * velocity_old + outer_grad
    engine_piece = (params - outer_rate * (outer_grad + outer_momentum * velocity)).astype(
        jnp.bfloat16
    )
    block = lax.all_gather(engine_piece, "rep", axis=1, tiled=True)
    engine = lax.all_to_all(block, "ep", split_axis=0, concat_axis=1, tiled=True)
    step_count = hidden.shape[0]
    inv_root = 1.0 / math.sqrt(model_width)
    tables = [
        routing_tables(expert_ids[step_index], gate_weights[step_index], experts, CAP)
        for step_index in range(step_count)
    ]
    outgoing = [
        jnp.dot(tables[step_index][0], hidden[step_index], preferred_element_type=jnp.float32)
        .astype(jnp.bfloat16)
        .reshape(owners, owned_count, CAP, model_width)
        for step_index in range(step_count)
    ]
    results = []
    for step_index in range(step_count):
        product = jnp.einsum(
            "pecd,edf->pecf",
            lax.all_to_all(outgoing[step_index], "ep", split_axis=0, concat_axis=0, tiled=True),
            engine,
            preferred_element_type=jnp.float32,
        )
        answered = jax.nn.silu(product * inv_root).astype(jnp.bfloat16)
        returned = lax.all_to_all(answered, "ep", split_axis=0, concat_axis=0, tiled=True)
        results.append(
            weigh_back(tables[step_index][1], returned.reshape(experts * CAP, hidden_width))
        )
    decoded = jnp.stack(results)
    return (engine, velocity.reshape(momentum.shape), decoded)


def solution(mesh):
    return jax.shard_map(
        local,
        mesh=mesh,
        in_specs=(
            P("rep", None, "ep", None),
            P(None, "ep", "rep", None, None),
            P(None, "ep", "rep", None, None),
            P(None, ("rep", "ep"), None),
            P(None, ("rep", "ep"), None),
            P(None, ("rep", "ep"), None),
        ),
        out_specs=(
            P("ep", None, None),
            P(None, "ep", "rep", None, None),
            P(None, ("rep", "ep"), None),
        ),
        check_vma=False,
    )
```

profile of v0, /device:TPU:2, one launch (start us, length us, event | category | flops | bytes accessed | tf_op | source)
XLA Modules:
  0.0 522.7 jit_solution(14840717370469638514)
XLA Ops:
  7.2 3.8 copy.105
  11.0 0.7 copy-done.3
  12.0 0.6 reduce-window.26
  12.6 0.2 slice_reduce_fusion.3
  13.0 0.2 fusion.53
  13.2 0.6 convolution_convert_fusion.3
  13.8 1.6 reshape.232
  15.5 14.8 %all-to-all-start.1 = ((bf16[64,1,6,2048]{3,2,1,0:T(8,128)(2,1)}), bf16[64,1,6,2048]{3,2,1,0:T(8,128)(2,1)}, u32[]{:S(2)}, u32[]{:S(2)}) async-start(bf16[64,1,6,2048]{3,2,1,0:T(8,128)(2,1)} %bitcast.13), calls=%async_computation.1 | async-start | bytes 4194304 | tf_op jit(solution)/shard_map/all_to_all | solution.py:71
  30.6 0.6 reduce-window.30
  31.2 0.2 slice_reduce_fusion.2
  31.7 0.2 fusion.52
  31.9 0.6 convolution_convert_fusion.2
  32.5 1.7 reshape.236
  34.2 70.6 %all-to-all-done.1 = bf16[64,1,6,2048]{3,2,1,0:T(8,128)(2,1)} async-done(((bf16[64,1,6,2048]{3,2,1,0:T(8,128)(2,1)}), bf16[64,1,6,2048]{3,2,1,0:T(8,128)(2,1)}, u32[]{:S(2)}, u32[]{:S(2)}) %all-to-all-start.1) | async-done | bytes 1572896 | tf_op jit(solution)/shard_map/all_to_all | solution.py:71
  104.8 6.5 %all-to-all-start.3 = ((bf16[64,1,6,2048]{3,2,1,0:T(8,128)(2,1)}), bf16[64,1,6,2048]{3,2,1,0:T(8,128)(2,1)}, u32[]{:S(2)}, u32[]{:S(2)}) async-start(bf16[64,1,6,2048]{3,2,1,0:T(8,128)(2,1)} %bitcast.24), calls=%async_computation.3 | async-start | bytes 4194304 | tf_op jit(solution)/shard_map/all_to_all | solution.py:71
  111.4 1.4 copy.155
  112.8 0.2 copy-done
  112.9 2.3 fusion.37
  115.5 0.6 reduce-window.34
  116.1 0.2 slice_reduce_fusion.1
  116.6 0.2 fusion.51
  116.8 2.7 convolution_convert_fusion.1
  119.4 2.5 reshape.240
  121.9 57.4 %all-to-all-done.3 = bf16[64,1,6,2048]{3,2,1,0:T(8,128)(2,1)} async-done(((bf16[64,1,6,2048]{3,2,1,0:T(8,128)(2,1)}), bf16[64,1,6,2048]{3,2,1,0:T(8,128)(2,1)}, u32[]{:S(2)}, u32[]{:S(2)}) %all-to-all-start.3) | async-done | bytes 1572896 | tf_op jit(solution)/shard_map/all_to_all | solution.py:71
  179.4 54.7 %all_to_all.52 = bf16[64,1,6,2048]{3,2,1,0:T(8,128)(2,1)} all-to-all(bf16[64,1,6,2048]{3,2,1,0:T(8,128)(2,1)S(1)} %bitcast.238), channel_id=1, replica_groups=mesh['rep'=4,'ep'=64] {'ep'}, dimensions={0} | all-to-all | bytes 3145728 | tf_op jit(solution)/shard_map/all_to_all | solution.py:71
  234.1 6.7 %all-to-all-start = ((bf16[64,32,768]{2,1,0:T(8,128)(2,1)}), bf16[64,32,768]{2,1,0:T(8,128)(2,1)S(1)}, u32[]{:S(2)}, u32[]{:S(2)}) async-start(bf16[64,32,768]{2,1,0:T(8,128)(2,1)} %all-gather.2.cloned.1.call-done), calls=%async_computation | async-start | bytes 6291456 | tf_op jit(solution)/shard_map/all_to_all | solution.py:54
  241.1 0.6 reduce-window.36
  241.7 0.2 slice_reduce_fusion
  242.2 0.2 fusion.50
  242.4 2.7 convolution_convert_fusion
  245.1 3.7 reshape.244
  248.7 62.8 %all-to-all-done = bf16[64,32,768]{2,1,0:T(8,128)(2,1)S(1)} async-done(((bf16[64,32,768]{2,1,0:T(8,128)(2,1)}), bf16[64,32,768]{2,1,0:T(8,128)(2,1)S(1)}, u32[]{:S(2)}, u32[]{:S(2)}) %all-to-all-start) | async-done | bytes 3145760 | tf_op jit(solution)/shard_map/all_to_all | solution.py:54
  311.5 41.4 %all-to-all-start.7 = ((bf16[64,1,6,2048]{3,2,1,0:T(8,128)(2,1)}), bf16[64,1,6,2048]{3,2,1,0:T(8,128)(2,1)}, u32[]{:S(2)}, u32[]{:S(2)}) async-start(bf16[64,1,6,2048]{3,2,1,0:T(8,128)(2,1)} %bitcast.237), calls=%async_computation.7 | async-start | bytes 4194304 | tf_op jit(solution)/shard_map/all_to_all | solution.py:71
  352.9 3.7 multiply_convert_fusion.3
  356.5 1.2 copy.75
  357.8 40.4 %all-to-all-done.7 = bf16[64,1,6,2048]{3,2,1,0:T(8,128)(2,1)} async-done(((bf16[64,1,6,2048]{3,2,1,0:T(8,128)(2,1)}), bf16[64,1,6,2048]{3,2,1,0:T(8,128)(2,1)}, u32[]{:S(2)}, u32[]{:S(2)}) %all-to-all-start.7) | async-done | bytes 1572896 | tf_op jit(solution)/shard_map/all_to_all | solution.py:71
  398.2 7.4 %all-to-all-start.2 = ((bf16[64,1,6,768]{3,2,1,0:T(8,128)(2,1)}), bf16[64,1,6,768]{3,2,1,0:T(8,128)(2,1)}, u32[]{:S(2)}, u32[]{:S(2)}) async-start(bf16[64,1,6,768]{3,2,1,0:T(8,128)(2,1)} %copy.75), calls=%async_computation.2 | async-start | bytes 1572864 | tf_op jit(solution)/shard_map/all_to_all | solution.py:76
  405.6 3.7 multiply_convert_fusion.2
  409.3 1.2 copy.81
  410.5 15.4 %all-to-all-done.2 = bf16[64,1,6,768]{3,2,1,0:T(8,128)(2,1)} async-done(((bf16[64,1,6,768]{3,2,1,0:T(8,128)(2,1)}), bf16[64,1,6,768]{3,2,1,0:T(8,128)(2,1)}, u32[]{:S(2)}, u32[]{:S(2)}) %all-to-all-start.2) | async-done | bytes 589856 | tf_op jit(solution)/shard_map/all_to_all | solution.py:76
  425.9 9.9 %all-to-all-start.4 = ((bf16[64,1,6,768]{3,2,1,0:T(8,128)(2,1)}), bf16[64,1,6,768]{3,2,1,0:T(8,128)(2,1)}, u32[]{:S(2)}, u32[]{:S(2)}) async-start(bf16[64,1,6,768]{3,2,1,0:T(8,128)(2,1)} %copy.81), calls=%async_computation.4 | async-start | bytes 1572864 | tf_op jit(solution)/shard_map/all_to_all | solution.py:76
  435.8 3.7 multiply_convert_fusion.1
  439.5 1.2 copy.87
  440.7 13.8 %all-to-all-done.4 = bf16[64,1,6,768]{3,2,1,0:T(8,128)(2,1)} async-done(((bf16[64,1,6,768]{3,2,1,0:T(8,128)(2,1)}), bf16[64,1,6,768]{3,2,1,0:T(8,128)(2,1)}, u32[]{:S(2)}, u32[]{:S(2)}) %all-to-all-start.4) | async-done | bytes 589856 | tf_op jit(solution)/shard_map/all_to_all | solution.py:76
  454.5 10.5 %all-to-all-start.6 = ((bf16[64,1,6,768]{3,2,1,0:T(8,128)(2,1)}), bf16[64,1,6,768]{3,2,1,0:T(8,128)(2,1)}, u32[]{:S(2)}, u32[]{:S(2)}) async-start(bf16[64,1,6,768]{3,2,1,0:T(8,128)(2,1)} %copy.87), calls=%async_computation.6 | async-start | bytes 1572864 | tf_op jit(solution)/shard_map/all_to_all | solution.py:76
  465.1 3.7 multiply_convert_fusion
  468.8 1.2 copy.93
  470.0 16.6 %all-to-all-done.6 = bf16[64,1,6,768]{3,2,1,0:T(8,128)(2,1)} async-done(((bf16[64,1,6,768]{3,2,1,0:T(8,128)(2,1)}), bf16[64,1,6,768]{3,2,1,0:T(8,128)(2,1)}, u32[]{:S(2)}, u32[]{:S(2)}) %all-to-all-start.6) | async-done | bytes 589856 | tf_op jit(solution)/shard_map/all_to_all | solution.py:76
  486.6 6.6 %all-to-all-start.8 = ((bf16[64,1,6,768]{3,2,1,0:T(8,128)(2,1)}), bf16[64,1,6,768]{3,2,1,0:T(8,128)(2,1)}, u32[]{:S(2)}, u32[]{:S(2)}) async-start(bf16[64,1,6,768]{3,2,1,0:T(8,128)(2,1)} %copy.93), calls=%async_computation.8 | async-start | bytes 1572864 | tf_op jit(solution)/shard_map/all_to_all | solution.py:76
  493.5 0.2 select_reduce_fusion.3
  493.7 0.2 select_reduce_fusion.2
  493.9 0.2 select_reduce_fusion.1
  494.1 0.2 select_reduce_fusion
  494.3 2.1 reshape.234
  496.4 2.1 reshape.238
  498.4 2.1 reshape.242
  500.5 1.4 fusion.38
  501.9 1.4 fusion.39
  503.4 1.4 fusion.40
  504.8 5.2 all-to-all-done.8
  510.0 2.1 reshape.246
  512.0 1.4 fusion.41
  513.5 0.7 pad_maximum_fusion
  514.2 1.7 copy.157
  (56 shorter events, 2.5 us)
Async XLA Ops:
  7.2 104.2 %reduce-scatter.4.cloned.1.call-start = ((), (), s32[]{:S(2)}) async-start(), calls=%async_computation.11 | async-start | bytes 3932160
  11.0 0.7 copy-start.3
  11.0 2.2 copy-start.2
  15.5 89.3 %all-to-all-start.1 = ((bf16[64,1,6,2048]{3,2,1,0:T(8,128)(2,1)}), bf16[64,1,6,2048]{3,2,1,0:T(8,128)(2,1)}, u32[]{:S(2)}, u32[]{:S(2)}) async-start(bf16[64,1,6,2048]{3,2,1,0:T(8,128)(2,1)} %bitcast.13), calls=%async_computation.1 | async-start | bytes 4194304 | tf_op jit(solution)/shard_map/all_to_all | solution.py:71
  104.8 8.0 %copy-start.1 = (f32[64,1,1,8,768]{4,3,2,1,0:T(8,128)S(1)}, f32[64,1,1,8,768]{4,3,2,1,0:T(8,128)}, u32[]{:S(2)}) copy-start(f32[64,1,1,8,768]{4,3,2,1,0:T(8,128)} %param.7) | copy-start | bytes 4718596
  104.8 74.6 %all-to-all-start.3 = ((bf16[64,1,6,2048]{3,2,1,0:T(8,128)(2,1)}), bf16[64,1,6,2048]{3,2,1,0:T(8,128)(2,1)}, u32[]{:S(2)}, u32[]{:S(2)}) async-start(bf16[64,1,6,2048]{3,2,1,0:T(8,128)(2,1)} %bitcast.24), calls=%async_computation.3 | async-start | bytes 4194304 | tf_op jit(solution)/shard_map/all_to_all | solution.py:71
  111.3 1.6 copy-start
  111.3 122.8 %all-gather.2.cloned.1.call-start = ((), (), s32[]{:S(2)}) async-start(), calls=%async_computation.10 | async-start | bytes 3932160 | tf_op jit(solution)/shard_map/all_gather | solution.py:53
  234.1 77.4 %all-to-all-start = ((bf16[64,32,768]{2,1,0:T(8,128)(2,1)}), bf16[64,32,768]{2,1,0:T(8,128)(2,1)S(1)}, u32[]{:S(2)}, u32[]{:S(2)}) async-start(bf16[64,32,768]{2,1,0:T(8,128)(2,1)} %all-gather.2.cloned.1.call-done), calls=%async_computation | async-start | bytes 6291456 | tf_op jit(solution)/shard_map/all_to_all | solution.py:54
  311.5 86.7 %all-to-all-start.7 = ((bf16[64,1,6,2048]{3,2,1,0:T(8,128)(2,1)}), bf16[64,1,6,2048]{3,2,1,0:T(8,128)(2,1)}, u32[]{:S(2)}, u32[]{:S(2)}) async-start(bf16[64,1,6,2048]{3,2,1,0:T(8,128)(2,1)} %bitcast.237), calls=%async_computation.7 | async-start | bytes 4194304 | tf_op jit(solution)/shard_map/all_to_all | solution.py:71
  398.2 27.7 %all-to-all-start.2 = ((bf16[64,1,6,768]{3,2,1,0:T(8,128)(2,1)}), bf16[64,1,6,768]{3,2,1,0:T(8,128)(2,1)}, u32[]{:S(2)}, u32[]{:S(2)}) async-start(bf16[64,1,6,768]{3,2,1,0:T(8,128)(2,1)} %copy.75), calls=%async_computation.2 | async-start | bytes 1572864 | tf_op jit(solution)/shard_map/all_to_all | solution.py:76
  425.9 28.6 %all-to-all-start.4 = ((bf16[64,1,6,768]{3,2,1,0:T(8,128)(2,1)}), bf16[64,1,6,768]{3,2,1,0:T(8,128)(2,1)}, u32[]{:S(2)}, u32[]{:S(2)}) async-start(bf16[64,1,6,768]{3,2,1,0:T(8,128)(2,1)} %copy.81), calls=%async_computation.4 | async-start | bytes 1572864 | tf_op jit(solution)/shard_map/all_to_all | solution.py:76
  454.5 32.1 %all-to-all-start.6 = ((bf16[64,1,6,768]{3,2,1,0:T(8,128)(2,1)}), bf16[64,1,6,768]{3,2,1,0:T(8,128)(2,1)}, u32[]{:S(2)}, u32[]{:S(2)}) async-start(bf16[64,1,6,768]{3,2,1,0:T(8,128)(2,1)} %copy.87), calls=%async_computation.6 | async-start | bytes 1572864 | tf_op jit(solution)/shard_map/all_to_all | solution.py:76
  468.8 24.4 %copy-start.4 = (f32[4,32,8]{1,2,0:T(8,128)S(1)}, f32[4,32,8]{1,2,0:T(8,128)}, u32[]{:S(2)}) copy-start(f32[4,32,8]{1,2,0:T(8,128)} %param.11) | copy-start | bytes 12292
  486.6 23.4 %all-to-all-start.8 = ((bf16[64,1,6,768]{3,2,1,0:T(8,128)(2,1)}), bf16[64,1,6,768]{3,2,1,0:T(8,128)(2,1)}, u32[]{:S(2)}, u32[]{:S(2)}) async-start(bf16[64,1,6,768]{3,2,1,0:T(8,128)(2,1)} %copy.93), calls=%async_computation.8 | async-start | bytes 1572864 | tf_op jit(solution)/shard_map/all_to_all | solution.py:76
Sparse Core Ops, SparseCore 0:
  11.1 84.4 reduce-scatter.3
  115.4 77.8 all-gather.1
where the time goes:
time: 524 us; the launch traced here: 523 us
  waiting for transfers between devices  282 us (54%)
  starting transfers between devices  104 us (20%)
  blocking collectives  54.7 us (10%)
  local copies, waits for them, and re-layouts  32.7 us (6%)
  matrix products  27.1 us (5%)
  between operations  14.4 us (3%)
  other arithmetic  7.62 us (1%)
    all_to_all x3, waiting for transfers between devices, local(): lax.all_to_all(outgoing[step_index], 'ep', split_axis=0, concat_axis=0, t...  168 us
    all_to_all x1, waiting for transfers between devices, local(): lax.all_to_all(block, 'ep', split_axis=0, concat_axis=1, tiled=True)  62.8 us
    all_to_all x3, starting transfers between devices, local(): lax.all_to_all(outgoing[step_index], 'ep', split_axis=0, concat_axis=0, t...  62.7 us
    all_to_all x1, blocking collectives, local(): lax.all_to_all(outgoing[step_index], 'ep', split_axis=0, concat_axis=0, t...  54.7 us
    all_to_all x4, waiting for transfers between devices, local(): lax.all_to_all(answered, 'ep', split_axis=0, concat_axis=0, tiled=True)  51 us
    all_to_all x4, starting transfers between devices, local(): lax.all_to_all(answered, 'ep', split_axis=0, concat_axis=0, tiled=True)  34.4 us
    dot_general x4, matrix products, local(): jnp.einsum('pecd,edf->pecf', lax.all_to_all(outgoing[step_index], 'ep', s...  14.7 us
  transfers between devices with their start and end apart: 10, of which 8 were waited for; matrix products, arithmetic and copies ran while one was open for 11% of the time, Pallas kernels for 0%

commit v1 on v0

v1 whole, which is shorter than its diff:
```python
import math

import jax
import jax.numpy as jnp
from jax import lax
from jax.sharding import Mesh, PartitionSpec as P

outer_momentum = 0.9
outer_rate = 0.7

RING = 4
PLUS = [(i, (i + 1) % RING) for i in range(RING)]
MINUS = [(i, (i - 1) % RING) for i in range(RING)]
SWAP = [(0, 1), (1, 0)]


def swap(value, axis):
    return lax.ppermute(value, axis, SWAP)


def ring_gather(value, axis):
    half = value.shape[0] // 2
    before = lax.ppermute(value, axis, PLUS)
    after = lax.ppermute(value, axis, MINUS)
    far_low = lax.ppermute(before[:half], axis, PLUS)
    far_high = lax.ppermute(after[half:], axis, MINUS)
    return value, before, after, (far_low, far_high)


def ring_scatter(own, before, after, far, axis):
    half = far.shape[0] // 2
    low = lax.ppermute(far[:half].astype(jnp.bfloat16), axis, PLUS)
    high = lax.ppermute(far[half:].astype(jnp.bfloat16), axis, MINUS)
    after = jnp.concatenate([after[:half] + low.astype(jnp.float32), after[half:]])
    before = jnp.concatenate([before[:half], before[half:] + high.astype(jnp.float32)])
    from_before = lax.ppermute(after.astype(jnp.bfloat16), axis, PLUS)
    from_after = lax.ppermute(before.astype(jnp.bfloat16), axis, MINUS)
    return own + from_before.astype(jnp.float32) + from_after.astype(jnp.float32)


def in_order(position, mine, other, axis):
    return jnp.where(
        position == 0,
        jnp.stack([mine, other], axis=axis),
        jnp.stack([other, mine], axis=axis),
    )


def at_offsets(value, position, axis):
    order = (position + jnp.array([0, 3, 1, 2], jnp.int32)) % RING
    return jnp.take(value, order, axis=axis)


def local(deltas, master, momentum, hidden, expert_ids, gate_weights):
    experts, block_rows, width = deltas.shape[1:]
    sub = master.shape[3]
    steps, rows, model = hidden.shape
    top = expert_ids.shape[2]
    z_lo, core = lax.axis_index("z_lo"), lax.axis_index("core")
    y, x, z_hi = lax.axis_index("y"), lax.axis_index("x"), lax.axis_index("z_hi")
    half_width = width // 2
    taken = steps * rows

    pieces = deltas[0].reshape(experts, 2, 2, sub, width)
    kept = lax.dynamic_index_in_dim(pieces, core, axis=2, keepdims=False)
    given = lax.dynamic_index_in_dim(pieces, 1 - core, axis=2, keepdims=False)
    pair = kept.astype(jnp.float32) + swap(given, "core").astype(jnp.float32)
    kept = lax.dynamic_index_in_dim(pair, z_lo, axis=1, keepdims=False)
    given = lax.dynamic_index_in_dim(pair, 1 - z_lo, axis=1, keepdims=False)
    summed = kept + swap(given.astype(jnp.bfloat16), "z_lo").astype(jnp.float32)
    params = master.reshape(experts, sub, width)
    velocity_old = momentum.reshape(experts, sub, width)
    outer_grad = summed / 4
    velocity = outer_momentum * velocity_old + outer_grad
    piece = (params - outer_rate * (outer_grad + outer_momentum * velocity)).astype(jnp.bfloat16)

    mine = lax.all_to_all(piece, ("y", "x", "z_hi"), split_axis=0, concat_axis=0, tiled=True)
    mine = in_order(z_lo, mine, swap(mine, "z_lo"), 1)
    mine = in_order(core, mine, swap(mine, "core"), 2)
    engine = mine.reshape(model, width)

    part = lax.dynamic_slice_in_dim(engine, core * half_width, half_width, axis=1)
    own, before, after, far = ring_gather(part, "x")
    weights = [own, before, after, jnp.concatenate(far)]
    offsets = [0, 3, 1, 2]

    flat = hidden.reshape(taken, model)
    own, before, after, far = ring_gather(flat, "z_hi")
    plane = jnp.concatenate([own, before, after, *far])
    own, before, after, far = ring_gather(plane, "y")
    plane = jnp.concatenate([own, before, after, *far])
    plane = jnp.concatenate([plane, swap(plane, "core")])

    routes = jnp.concatenate([expert_ids.astype(jnp.float32), gate_weights], axis=-1)
    routes = routes.reshape(taken, 2 * top)
    routes = lax.all_gather(routes, ("core", "y", "z_hi"), axis=0).reshape(2, RING, RING, taken, 2 * top)
    routes = jnp.take(routes, (core + jnp.arange(2, dtype=jnp.int32)) % 2, axis=0)
    routes = at_offsets(at_offsets(routes, y, 1), z_hi, 2).reshape(-1, 2 * top)
    ids, gates = routes[:, :top].astype(jnp.int32), routes[:, top:]

    total = None
    inv_root = 1.0 / math.sqrt(model)
    for offset, weight in zip(offsets, weights):
        expert = (y * RING + (x + offset) % RING) * RING + z_hi
        gate = jnp.sum(jnp.where(ids == expert, gates, 0.0), axis=1)
        product = jnp.dot(plane, weight, preferred_element_type=jnp.float32)
        answer = jax.nn.silu(product * inv_root).astype(jnp.bfloat16).astype(jnp.float32)
        term = gate[:, None] * answer
        total = term if total is None else total + term

    total = total.reshape(2, RING, RING, taken, half_width).transpose(1, 2, 0, 3, 4)
    total = total.reshape(RING, RING, 2 * taken, half_width)
    ringed = ring_scatter(
        *[total[i].reshape(RING * 2 * taken, half_width) for i in range(RING)], "y"
    ).reshape(RING, 2 * taken, half_width)
    ringed = ring_scatter(*[ringed[i] for i in range(RING)], "z_hi").reshape(2, taken, half_width)
    mine, other = ringed[0], swap(ringed[1].astype(jnp.bfloat16), "core").astype(jnp.float32)
    decoded = in_order(core, mine, other, 1).reshape(steps, rows, width).astype(jnp.bfloat16)
    return (engine[None], velocity.reshape(momentum.shape), decoded)


def solution(mesh):
    fine = Mesh(
        mesh.devices.reshape(2, 2, RING, RING, RING), ("z_lo", "core", "y", "x", "z_hi")
    )
    rep, ep = ("z_lo", "core"), ("y", "x", "z_hi")
    return jax.shard_map(
        local,
        mesh=fine,
        in_specs=(
            P(rep, None, ep, None),
            P(None, ep, rep, None, None),
            P(None, ep, rep, None, None),
            P(None, rep + ep, None),
            P(None, rep + ep, None),
            P(None, rep + ep, None),
        ),
        out_specs=(
            P(ep, None, None),
            P(None, ep, rep, None, None),
            P(None, rep + ep, None),
        ),
        check_vma=False,
    )
```

time: 524 us -> 460 us (0.88)
  the two profiles are of different devices: /device:TPU:2 before, /device:TPU:1 now
where the time goes in v1:
time: 460 us; the launch traced here: 456 us
  waiting for transfers between devices  178 us (39%)
  blocking collectives  106 us (23%)
  matrix products  64.6 us (14%)
  starting transfers between devices  56.8 us (12%)
  local copies, waits for them, and re-layouts  37.5 us (8%)
  other arithmetic  11.4 us (2%)
    ppermute x3, waiting for transfers between devices, ring_gather(): before = lax.ppermute(value, axis, PLUS)  91.4 us
    all_gather x1, blocking collectives, local(): lax.all_gather(routes, ('core', 'y', 'z_hi'), axis=0)  72.6 us
    dot_general x4, matrix products, local(): product = jnp.dot(plane, weight, preferred_element_type=jnp.float32)  64.6 us
    ppermute x6, waiting for transfers between devices, swap(): return lax.ppermute(value, axis, SWAP)  37.1 us
    all_to_all x1, blocking collectives, local(): lax.all_to_all(piece, ('y', 'x', 'z_hi'), split_axis=0, concat_axis=0, ti...  33.2 us
    ppermute x2, waiting for transfers between devices, ring_scatter(): from_before = lax.ppermute(after.astype(jnp.bfloat16), axis, PLUS)  18.7 us
    unnamed x22, local copies, waits for them, and re-layouts  15 us
    ppermute x3, waiting for transfers between devices, ring_gather(): far_low = lax.ppermute(before[:half], axis, PLUS)  14.9 us
  transfers between devices with their start and end apart: 26, of which 15 were waited for; matrix products, arithmetic and copies ran while one was open for 21% of the time, Pallas kernels for 0%

profile of v1, /device:TPU:1, one launch (start us, length us, event | category | flops | bytes accessed | tf_op | source)
XLA Modules:
  0.0 455.6 jit_solution(17420329998775129565)
XLA Ops:
  0.6 3.9 collective-permute-start.4
  4.5 3.1 collective-permute-start.5
  7.6 2.4 constant_dynamic-update-slice_fusion.13
  10.0 13.5 %collective-permute-done.4 = bf16[128,2048]{1,0:T(8,128)(2,1)S(1)} collective-permute-done((bf16[128,2048]{1,0:T(8,128)(2,1)}, bf16[128,2048]{1,0:T(8,128)(2,1)S(1)}, u32[]{:S(2)}, u32[]{:S(2)}) %collective-permute-start.4) | collective-permute-done | bytes 524320 | tf_op jit(solution)/shard_map/ppermute | solution.py:23
  23.5 7.9 %collective-permute-start.6 = (bf16[64,2048]{1,0:T(8,128)(2,1)S(1)}, bf16[64,2048]{1,0:T(8,128)(2,1)S(1)}, u32[]{:S(2)}, u32[]{:S(2)}) collective-permute-start(bf16[64,2048]{1,0:T(8,128)(2,1)S(1)} %slice.162), channel_id=1, source_target_pairs={{0,1},{1,2},{2,3},{3,0},{4,5},{5,6},{6,7},{7,4},{8,9},{9,10},{10,1... | collective-permute-start | bytes 786440 | tf_op jit(solution)/shard_map/ppermute | solution.py:25
  31.5 0.7 collective-permute-done.5
  32.1 2.4 collective-permute-start.7
  34.6 1.3 constant_dynamic-update-slice_fusion.12
  35.9 1.3 constant_dynamic-update-slice_fusion.11
  37.3 2.5 collective-permute-done.6
  39.8 1.0 constant_dynamic-update-slice_fusion.10
  40.7 6.2 %collective-permute-done.7 = bf16[64,2048]{1,0:T(8,128)(2,1)S(1)} collective-permute-done((bf16[64,2048]{1,0:T(8,128)(2,1)S(1)}, bf16[64,2048]{1,0:T(8,128)(2,1)S(1)}, u32[]{:S(2)}, u32[]{:S(2)}) %collective-permute-start.7) | collective-permute-done | bytes 262176 | tf_op jit(solution)/shard_map/ppermute | solution.py:26
  46.9 1.0 constant_dynamic-update-slice_fusion.9
  47.8 1.3 collective-permute-start.8
  49.1 1.4 collective-permute-start.9
  50.6 45.5 %collective-permute-done.8 = bf16[512,2048]{1,0:T(8,128)(2,1)S(1)} collective-permute-done((bf16[512,2048]{1,0:T(8,128)(2,1)}, bf16[512,2048]{1,0:T(8,128)(2,1)S(1)}, u32[]{:S(2)}, u32[]{:S(2)}) %collective-permute-start.8) | collective-permute-done | bytes 2097184 | tf_op jit(solution)/shard_map/ppermute | solution.py:23
  96.1 1.4 copy-done.1
  97.5 1.0 slice.164
  98.6 2.7 collective-permute-start.11
  101.4 2.7 dynamic-slice_bitcast_fusion
  104.0 1.8 collective-permute-start
  105.9 2.5 constant_dynamic-update-slice_fusion.8
  108.3 2.5 constant_dynamic-update-slice_fusion.7
  110.9 12.4 %collective-permute-done.10 = bf16[256,2048]{1,0:T(8,128)(2,1)S(1)} collective-permute-done((bf16[256,2048]{1,0:T(8,128)(2,1)}, bf16[256,2048]{1,0:T(8,128)(2,1)S(1)}, u32[]{:S(2)}, u32[]{:S(2)}) %collective-permute-start.10) | collective-permute-done | bytes 1048608 | tf_op jit(solution)/shard_map/ppermute | solution.py:25
  123.3 1.5 constant_dynamic-update-slice_fusion.6
  124.8 1.7 constant_dynamic-update-slice_fusion.5
  126.5 2.2 collective-permute-start.12
  128.7 2.3 convert_add_fusion
  131.0 1.0 fusion.6
  132.0 19.5 %collective-permute-done.1 = bf16[64,8,768]{2,1,0:T(8,128)(2,1)} collective-permute-done((bf16[64,8,768]{2,1,0:T(8,128)(2,1)}, bf16[64,8,768]{2,1,0:T(8,128)(2,1)}, u32[]{:S(2)}, u32[]{:S(2)}) %collective-permute-start.1) | collective-permute-done | bytes 786464 | tf_op jit(solution)/shard_map/ppermute | solution.py:18
  151.5 3.7 fusion.11
  155.3 33.2 %all_to_all.5 = bf16[64,8,768]{2,1,0:T(8,128)(2,1)S(1)} all-to-all(bf16[64,8,768]{2,1,0:T(8,128)(2,1)S(1)} %get-tuple-element.25), channel_id=1, replica_groups=mesh['z_lo'=2,'core'=2,'y'=4,'x'=4,'z_hi'=4] {'y','x','z_hi'}, dimensions={0} | all-to-all | bytes 1572864 | tf_op jit(solution)/shard_map/all_to_all | solution.py:77
  188.7 16.6 %collective-permute-done.2 = bf16[64,8,768]{2,1,0:T(8,128)(2,1)S(1)} collective-permute-done((bf16[64,8,768]{2,1,0:T(8,128)(2,1)S(1)}, bf16[64,8,768]{2,1,0:T(8,128)(2,1)S(1)}, u32[]{:S(2)}, u32[]{:S(2)}) %collective-permute-start.2) | collective-permute-done | bytes 786464 | tf_op jit(solution)/shard_map/ppermute | solution.py:18
  205.4 1.4 maximum_select_fusion.2
  206.8 3.3 collective-permute-start.3
  210.2 72.6 %all_gather.3 = f32[32,128,16]{1,2,0:T(8,128)S(1)} all-gather(f32[1,128,16]{1,2,0:T(8,128)S(1)} %all_gather_reshape.3), channel_id=1, replica_groups=mesh['z_lo'=2,'core'=2,'y'=4,'x'=4,'z_hi'=4] {'core','y','z_hi'}, dimensions={0}, use_global_device_ids=true | all-gather | bytes 270336 | tf_op jit(solution)/shard_map/all_gather | solution.py:96
  282.9 0.6 gather_fusion
  283.8 2.4 maximum_select_fusion
  286.9 2.7 collective-permute-start.14
  289.7 0.6 gather_fusion.1
  290.4 0.6 gather_fusion.2
  291.5 32.4 %collective-permute-done.13 = bf16[2048,384]{1,0:T(8,128)(2,1)} collective-permute-done((bf16[2048,384]{1,0:T(8,128)(2,1)S(1)}, bf16[2048,384]{1,0:T(8,128)(2,1)}, u32[]{:S(2)}, u32[]{:S(2)}) %collective-permute-start.13) | collective-permute-done | bytes 1572896 | tf_op jit(solution)/shard_map/ppermute | solution.py:23
  323.9 1.2 slice.166
  325.2 1.2 slice.167
  326.4 2.7 collective-permute-start.16
  329.2 8.3 %constant_dynamic-update-slice_fusion.14 = bf16[4096,2048]{1,0:T(8,128)(2,1)} fusion(bf16[4096,2048]{1,0:T(8,128)(2,1)} %get-tuple-element.37, bf16[2048,2048]{1,0:T(8,128)(2,1)} %collective-permute-done.12), kind=kLoop, calls=%fused_computation.73 | loop fusion | bytes 16777216 | tf_op jit(solution)/shard_map/concatenate | solution.py:92
  337.5 15.4 %multiply_convert_fusion.3 = bf16[4096,384]{1,0:T(8,128)(2,1)S(1)} fusion(bf16[4096,2048]{1,0:T(8,128)(2,1)} %constant_dynamic-update-slice_fusion.14, bf16[2048,384]{1,0:T(8,128)(2,1)S(1)} %constant_dynamic-slice_fusion), kind=kOutput, calls=%fused_computation.12 | convolution fusion | flops 6451888128 | bytes 21495808 | tf_op jit(solution)/shard_map/dot_general | solution.py:106
  352.9 12.7 %multiply_convert_fusion.2 = bf16[4096,384]{1,0:T(8,128)(2,1)} fusion(bf16[4096,2048]{1,0:T(8,128)(2,1)S(1)} %copy-done.4, bf16[2048,384]{1,0:T(8,128)(2,1)} %collective-permute-done.13), kind=kOutput, calls=%fused_computation.11 | convolution fusion | flops 6451888128 | bytes 21495808 | tf_op jit(solution)/shard_map/dot_general | solution.py:106
  365.7 21.3 %multiply_convert_fusion.1 = bf16[4096,384]{1,0:T(8,128)(2,1)} fusion(bf16[4096,2048]{1,0:T(8,128)(2,1)S(1)} %copy-done.4, bf16[2048,384]{1,0:T(8,128)(2,1)} %collective-permute-done.14), kind=kOutput, calls=%fused_computation.10 | convolution fusion | flops 6451888128 | bytes 21495808 | tf_op jit(solution)/shard_map/dot_general | solution.py:106
  387.0 15.1 %multiply_add_fusion = f32[4096,384]{1,0:T(8,128)S(1)} fusion(bf16[4096,384]{1,0:T(8,128)(2,1)} %multiply_convert_fusion.1, bf16[4096,384]{1,0:T(8,128)(2,1)} %multiply_convert_fusion.2, bf16[4096,384]{1,0:T(8,128)(2,1)S(1)} %multiply_convert_fusion.3, bf16[4096,2048]{1,0:T(8,128)(2,1)} %constant_dynamic-update-slice_fusion.14, ...), kind=kOutput, calls=%fused_computation.8 | convolution fusion | flops 6472335360 | bytes 34144256 | tf_op jit(solution)/shard_map/dot_general | solution.py:106
  402.1 0.5 copy.40
  402.9 0.7 copy.39
  403.6 2.7 collective-permute-start.19
  406.4 6.6 %collective-permute-done.17 = bf16[512,384]{1,0:T(8,128)(2,1)S(1)} collective-permute-done((bf16[512,384]{1,0:T(8,128)(2,1)S(1)}, bf16[512,384]{1,0:T(8,128)(2,1)S(1)}, u32[]{:S(2)}, u32[]{:S(2)}) %collective-permute-start.17) | collective-permute-done | bytes 393248 | tf_op jit(solution)/shard_map/ppermute | solution.py:32
  413.5 3.2 collective-permute-start.20
  416.7 14.2 %collective-permute-done.18 = bf16[1024,384]{1,0:T(8,128)(2,1)S(1)} collective-permute-done((bf16[1024,384]{1,0:T(8,128)(2,1)S(1)}, bf16[1024,384]{1,0:T(8,128)(2,1)S(1)}, u32[]{:S(2)}, u32[]{:S(2)}) %collective-permute-start.18) | collective-permute-done | bytes 786464 | tf_op jit(solution)/shard_map/ppermute | solution.py:36
  431.3 3.6 collective-permute-start.23
  434.9 2.0 collective-permute-done.21
  436.9 0.6 collective-permute-done.23
  437.7 4.2 collective-permute-start.24
  441.8 4.5 collective-permute-done.22
  446.5 6.9 %collective-permute-start.25 = (bf16[128,384]{1,0:T(8,128)(2,1)S(1)}, bf16[128,384]{1,0:T(8,128)(2,1)S(1)}, u32[]{:S(2)}, u32[]{:S(2)}) collective-permute-start(bf16[128,384]{1,0:T(8,128)(2,1)S(1)} %get-tuple-element.60), channel_id=1, source_target_pairs={{0,64},{64,0},{1,65},{65,1},{2,66},{66,2},{3,67},{67,3},{4,68},{68... | collective-permute-start | bytes 294920 | tf_op jit(solution)/shard_map/ppermute | solution.py:18
  453.4 0.9 collective-permute-done.25
  454.6 0.8 convert_element_type.125
  (72 shorter events, 4.2 us)
Async XLA Ops:
  0.6 22.9 %collective-permute-start.4 = (bf16[128,2048]{1,0:T(8,128)(2,1)}, bf16[128,2048]{1,0:T(8,128)(2,1)S(1)}, u32[]{:S(2)}, u32[]{:S(2)}) collective-permute-start(bf16[128,2048]{1,0:T(8,128)(2,1)} %bitcast.115), channel_id=1, source_target_pairs={{0,1},{1,2},{2,3},{3,0},{4,5},{5,6},{6,7},{7,4},{8,9},{9,10},{10,1... | collective-permute-start | bytes 1572872 | tf_op jit(solution)/shard_map/ppermute | solution.py:23
  4.5 27.6 %collective-permute-start.5 = (bf16[128,2048]{1,0:T(8,128)(2,1)}, bf16[128,2048]{1,0:T(8,128)(2,1)S(1)}, u32[]{:S(2)}, u32[]{:S(2)}) collective-permute-start(bf16[128,2048]{1,0:T(8,128)(2,1)} %bitcast.116), channel_id=1, source_target_pairs={{0,3},{1,0},{2,1},{3,2},{4,7},{5,4},{6,5},{7,6},{8,11},{9,8},{10,9... | collective-permute-start | bytes 1572872 | tf_op jit(solution)/shard_map/ppermute | solution.py:24
  23.5 16.2 %collective-permute-start.6 = (bf16[64,2048]{1,0:T(8,128)(2,1)S(1)}, bf16[64,2048]{1,0:T(8,128)(2,1)S(1)}, u32[]{:S(2)}, u32[]{:S(2)}) collective-permute-start(bf16[64,2048]{1,0:T(8,128)(2,1)S(1)} %slice.162), channel_id=1, source_target_pairs={{0,1},{1,2},{2,3},{3,0},{4,5},{5,6},{6,7},{7,4},{8,9},{9,10},{10,1... | collective-permute-start | bytes 786440 | tf_op jit(solution)/shard_map/ppermute | solution.py:25
  32.1 14.7 %collective-permute-start.7 = (bf16[64,2048]{1,0:T(8,128)(2,1)S(1)}, bf16[64,2048]{1,0:T(8,128)(2,1)S(1)}, u32[]{:S(2)}, u32[]{:S(2)}) collective-permute-start(bf16[64,2048]{1,0:T(8,128)(2,1)S(1)} %slice.163), channel_id=1, source_target_pairs={{0,3},{1,0},{2,1},{3,2},{4,7},{5,4},{6,5},{7,6},{8,11},{9,8},{10,9... | collective-permute-start | bytes 786440 | tf_op jit(solution)/shard_map/ppermute | solution.py:26
  47.8 48.2 %collective-permute-start.8 = (bf16[512,2048]{1,0:T(8,128)(2,1)}, bf16[512,2048]{1,0:T(8,128)(2,1)S(1)}, u32[]{:S(2)}, u32[]{:S(2)}) collective-permute-start(bf16[512,2048]{1,0:T(8,128)(2,1)} %get-tuple-element.55), channel_id=1, source_target_pairs={{0,16},{16,32},{32,48},{48,0},{1,17},{17,33},{33,49},{49,1},{2,18}... | collective-permute-start | bytes 6291464 | tf_op jit(solution)/shard_map/ppermute | solution.py:23
  49.1 49.4 %collective-permute-start.9 = (bf16[512,2048]{1,0:T(8,128)(2,1)}, bf16[512,2048]{1,0:T(8,128)(2,1)S(1)}, u32[]{:S(2)}, u32[]{:S(2)}) collective-permute-start(bf16[512,2048]{1,0:T(8,128)(2,1)} %get-tuple-element.55), channel_id=1, source_target_pairs={{0,48},{16,0},{32,16},{48,32},{1,49},{17,1},{33,17},{49,33},{2,50}... | collective-permute-start | bytes 6291464 | tf_op jit(solution)/shard_map/ppermute | solution.py:24
  96.1 1.4 copy-start.1
  98.5 24.8 %collective-permute-start.10 = (bf16[256,2048]{1,0:T(8,128)(2,1)}, bf16[256,2048]{1,0:T(8,128)(2,1)S(1)}, u32[]{:S(2)}, u32[]{:S(2)}) collective-permute-start(bf16[256,2048]{1,0:T(8,128)(2,1)} %slice.164), channel_id=1, source_target_pairs={{0,16},{16,32},{32,48},{48,0},{1,17},{17,33},{33,49},{49,1},{2,18}... | collective-permute-start | bytes 3145736 | tf_op jit(solution)/shard_map/ppermute | solution.py:25
  98.5 7.4 %copy-start.2 = (bf16[512,2048]{1,0:T(8,128)(2,1)S(1)}, bf16[512,2048]{1,0:T(8,128)(2,1)}, u32[]{:S(2)}) copy-start(bf16[512,2048]{1,0:T(8,128)(2,1)} %copy-done.1) | copy-start | bytes 6291460
  98.6 26.2 %collective-permute-start.11 = (bf16[256,2048]{1,0:T(8,128)(2,1)S(1)}, bf16[256,2048]{1,0:T(8,128)(2,1)S(1)}, u32[]{:S(2)}, u32[]{:S(2)}) collective-permute-start(bf16[256,2048]{1,0:T(8,128)(2,1)S(1)} %slice.165), channel_id=1, source_target_pairs={{0,48},{16,0},{32,16},{48,32},{1,49},{17,1},{33,17},{49,33},{2,50}... | collective-permute-start | bytes 3145736 | tf_op jit(solution)/shard_map/ppermute | solution.py:26
  104.0 24.7 %collective-permute-start = (bf16[64,2,8,768]{3,2,1,0:T(8,128)(2,1)}, bf16[64,2,8,768]{3,2,1,0:T(8,128)(2,1)}, u32[]{:S(2)}, u32[]{:S(2)}) collective-permute-start(bf16[64,2,8,768]{3,2,1,0:T(8,128)(2,1)} %dynamic-slice_bitcast_fusion), channel_id=1, source_target_pairs={{0,64},{64,0},{1,65},{65,1},{2,66},{66,2},{3,67},{67,3},{4,68},{68... | collective-permute-start | bytes 4718600 | tf_op jit(solution)/shard_map/ppermute | solution.py:18
  126.5 202.7 %collective-permute-start.12 = (bf16[2048,2048]{1,0:T(8,128)(2,1)}, bf16[2048,2048]{1,0:T(8,128)(2,1)}, u32[]{:S(2)}, u32[]{:S(2)}) collective-permute-start(bf16[2048,2048]{1,0:T(8,128)(2,1)} %get-tuple-element.36), channel_id=1, source_target_pairs={{0,64},{64,0},{1,65},{65,1},{2,66},{66,2},{3,67},{67,3},{4,68},{68... | collective-permute-start | bytes 25165832 | tf_op jit(solution)/shard_map/ppermute | solution.py:18
  132.0 19.5 %collective-permute-start.1 = (bf16[64,8,768]{2,1,0:T(8,128)(2,1)}, bf16[64,8,768]{2,1,0:T(8,128)(2,1)}, u32[]{:S(2)}, u32[]{:S(2)}) collective-permute-start(bf16[64,8,768]{2,1,0:T(8,128)(2,1)} %fusion.6), channel_id=1, source_target_pairs={{0,128},{128,0},{1,129},{129,1},{2,130},{130,2},{3,131},{131,3},{4... | collective-permute-start | bytes 2359304 | tf_op jit(solution)/shard_map/ppermute | solution.py:18
  155.3 54.8 %copy-start.3 = (s32[4,32,8]{1,2,0:T(8,128)S(1)}, s32[4,32,8]{1,2,0:T(8,128)}, u32[]{:S(2)}) copy-start(s32[4,32,8]{1,2,0:T(8,128)} %param.12) | copy-start | bytes 12292
  155.3 54.8 %copy-start.5 = (f32[4,32,8]{1,2,0:T(8,128)S(1)}, f32[4,32,8]{1,2,0:T(8,128)}, u32[]{:S(2)}) copy-start(f32[4,32,8]{1,2,0:T(8,128)} %param.13) | copy-start | bytes 12292
  188.5 16.9 %collective-permute-start.2 = (bf16[64,8,768]{2,1,0:T(8,128)(2,1)S(1)}, bf16[64,8,768]{2,1,0:T(8,128)(2,1)S(1)}, u32[]{:S(2)}, u32[]{:S(2)}) collective-permute-start(bf16[64,8,768]{2,1,0:T(8,128)(2,1)S(1)} %all_to_all.5), channel_id=1, source_target_pairs={{0,128},{128,0},{1,129},{129,1},{2,130},{130,2},{3,131},{131,3},{4... | collective-permute-start | bytes 2359304 | tf_op jit(solution)/shard_map/ppermute | solution.py:18
  206.8 76.7 %copy-start.6 = (s32[4]{0:T(128)S(1)}, s32[4]{0:T(128)}, u32[]{:S(2)}) copy-start(s32[4]{0:T(128)} %constant.152.clone) | copy-start | bytes 52
  206.8 77.0 %collective-permute-start.3 = (bf16[64,2,8,768]{3,2,0,1:T(8,128)(2,1)}, bf16[64,2,8,768]{3,2,0,1:T(8,128)(2,1)}, u32[]{:S(2)}, u32[]{:S(2)}) collective-permute-start(bf16[64,2,8,768]{3,2,0,1:T(8,128)(2,1)} %maximum_select_fusion.2), channel_id=1, source_target_pairs={{0,64},{64,0},{1,65},{65,1},{2,66},{66,2},{3,67},{67,3},{4,68},{68... | collective-permute-start | bytes 4718600 | tf_op jit(solution)/shard_map/ppermute | solution.py:18
  286.6 3.1 copy-start
  286.8 37.1 %collective-permute-start.13 = (bf16[2048,384]{1,0:T(8,128)(2,1)S(1)}, bf16[2048,384]{1,0:T(8,128)(2,1)}, u32[]{:S(2)}, u32[]{:S(2)}) collective-permute-start(bf16[2048,384]{1,0:T(8,128)(2,1)S(1)} %constant_dynamic-slice_fusion), channel_id=1, source_target_pairs={{0,4},{4,8},{8,12},{12,0},{1,5},{5,9},{9,13},{13,1},{2,6},{6,10},{... | collective-permute-start | bytes 4718600 | tf_op jit(solution)/shard_map/ppermute | solution.py:23
  286.9 38.3 %collective-permute-start.14 = (bf16[2048,384]{1,0:T(8,128)(2,1)S(1)}, bf16[2048,384]{1,0:T(8,128)(2,1)}, u32[]{:S(2)}, u32[]{:S(2)}) collective-permute-start(bf16[2048,384]{1,0:T(8,128)(2,1)S(1)} %constant_dynamic-slice_fusion), channel_id=1, source_target_pairs={{0,12},{4,0},{8,4},{12,8},{1,13},{5,1},{9,5},{13,9},{2,14},{6,2},{... | collective-permute-start | bytes 4718600 | tf_op jit(solution)/shard_map/ppermute | solution.py:24
  325.1 61.8 %collective-permute-start.15 = (bf16[1024,384]{1,0:T(8,128)(2,1)S(1)}, bf16[1024,384]{1,0:T(8,128)(2,1)S(1)}, u32[]{:S(2)}, u32[]{:S(2)}) collective-permute-start(bf16[1024,384]{1,0:T(8,128)(2,1)S(1)} %slice.166), channel_id=1, source_target_pairs={{0,4},{4,8},{8,12},{12,0},{1,5},{5,9},{9,13},{13,1},{2,6},{6,10},{... | collective-permute-start | bytes 2359304 | tf_op jit(solution)/shard_map/ppermute | solution.py:25
  326.4 60.5 %collective-permute-start.16 = (bf16[1024,384]{1,0:T(8,128)(2,1)S(1)}, bf16[1024,384]{1,0:T(8,128)(2,1)S(1)}, u32[]{:S(2)}, u32[]{:S(2)}) collective-permute-start(bf16[1024,384]{1,0:T(8,128)(2,1)S(1)} %slice.167), channel_id=1, source_target_pairs={{0,12},{4,0},{8,4},{12,8},{1,13},{5,1},{9,5},{13,9},{2,14},{6,2},{... | collective-permute-start | bytes 2359304 | tf_op jit(solution)/shard_map/ppermute | solution.py:26
  337.5 15.4 %copy-start.4 = (bf16[4096,2048]{1,0:T(8,128)(2,1)S(1)}, bf16[4096,2048]{1,0:T(8,128)(2,1)}, u32[]{:S(2)}) copy-start(bf16[4096,2048]{1,0:T(8,128)(2,1)} %constant_dynamic-update-slice_fusion.14) | copy-start | bytes 50331652
  402.8 10.2 %collective-permute-start.17 = (bf16[512,384]{1,0:T(8,128)(2,1)S(1)}, bf16[512,384]{1,0:T(8,128)(2,1)S(1)}, u32[]{:S(2)}, u32[]{:S(2)}) collective-permute-start(bf16[512,384]{1,0:T(8,128)(2,1)S(1)} %bitcast.119), channel_id=1, source_target_pairs={{0,16},{16,32},{32,48},{48,0},{1,17},{17,33},{33,49},{49,1},{2,18}... | collective-permute-start | bytes 1179656 | tf_op jit(solution)/shard_map/ppermute | solution.py:32
  403.6 9.7 %collective-permute-start.19 = (bf16[512,384]{1,0:T(8,128)(2,1)S(1)}, bf16[512,384]{1,0:T(8,128)(2,1)S(1)}, u32[]{:S(2)}, u32[]{:S(2)}) collective-permute-start(bf16[512,384]{1,0:T(8,128)(2,1)S(1)} %bitcast.118), channel_id=1, source_target_pairs={{0,48},{16,0},{32,16},{48,32},{1,49},{17,1},{33,17},{49,33},{2,50}... | collective-permute-start | bytes 1179656 | tf_op jit(solution)/shard_map/ppermute | solution.py:33
  413.2 17.7 %collective-permute-start.18 = (bf16[1024,384]{1,0:T(8,128)(2,1)S(1)}, bf16[1024,384]{1,0:T(8,128)(2,1)S(1)}, u32[]{:S(2)}, u32[]{:S(2)}) collective-permute-start(bf16[1024,384]{1,0:T(8,128)(2,1)S(1)} %pad_maximum_fusion), channel_id=1, source_target_pairs={{0,16},{16,32},{32,48},{48,0},{1,17},{17,33},{33,49},{49,1},{2,18}... | collective-permute-start | bytes 2359304 | tf_op jit(solution)/shard_map/ppermute | solution.py:36
  413.5 17.5 %collective-permute-start.20 = (bf16[1024,384]{1,0:T(8,128)(2,1)S(1)}, bf16[1024,384]{1,0:T(8,128)(2,1)S(1)}, u32[]{:S(2)}, u32[]{:S(2)}) collective-permute-start(bf16[1024,384]{1,0:T(8,128)(2,1)S(1)} %pad_maximum_fusion.1), channel_id=1, source_target_pairs={{0,48},{16,0},{32,16},{48,32},{1,49},{17,1},{33,17},{49,33},{2,50}... | collective-permute-start | bytes 2359304 | tf_op jit(solution)/shard_map/ppermute | solution.py:37
  431.2 5.7 %collective-permute-start.21 = (bf16[128,384]{1,0:T(8,128)(2,1)S(1)}, bf16[128,384]{1,0:T(8,128)(2,1)S(1)}, u32[]{:S(2)}, u32[]{:S(2)}) collective-permute-start(bf16[128,384]{1,0:T(8,128)(2,1)S(1)} %get-tuple-element.40), channel_id=1, source_target_pairs={{0,1},{1,2},{2,3},{3,0},{4,5},{5,6},{6,7},{7,4},{8,9},{9,10},{10,1... | collective-permute-start | bytes 294920 | tf_op jit(solution)/shard_map/ppermute | solution.py:32
  431.3 6.2 %collective-permute-start.23 = (bf16[128,384]{1,0:T(8,128)(2,1)S(1)}, bf16[128,384]{1,0:T(8,128)(2,1)S(1)}, u32[]{:S(2)}, u32[]{:S(2)}) collective-permute-start(bf16[128,384]{1,0:T(8,128)(2,1)S(1)} %get-tuple-element.41), channel_id=1, source_target_pairs={{0,3},{1,0},{2,1},{3,2},{4,7},{5,4},{6,5},{7,6},{8,11},{9,8},{10,9... | collective-permute-start | bytes 294920 | tf_op jit(solution)/shard_map/ppermute | solution.py:33
  437.6 8.8 %collective-permute-start.22 = (bf16[256,384]{1,0:T(8,128)(2,1)S(1)}, bf16[256,384]{1,0:T(8,128)(2,1)S(1)}, u32[]{:S(2)}, u32[]{:S(2)}) collective-permute-start(bf16[256,384]{1,0:T(8,128)(2,1)S(1)} %pad_maximum_fusion.2), channel_id=1, source_target_pairs={{0,1},{1,2},{2,3},{3,0},{4,5},{5,6},{6,7},{7,4},{8,9},{9,10},{10,1... | collective-permute-start | bytes 589832 | tf_op jit(solution)/shard_map/ppermute | solution.py:36
  437.7 8.7 %collective-permute-start.24 = (bf16[256,384]{1,0:T(8,128)(2,1)S(1)}, bf16[256,384]{1,0:T(8,128)(2,1)S(1)}, u32[]{:S(2)}, u32[]{:S(2)}) collective-permute-start(bf16[256,384]{1,0:T(8,128)(2,1)S(1)} %pad_maximum_fusion.3), channel_id=1, source_target_pairs={{0,3},{1,0},{2,1},{3,2},{4,7},{5,4},{6,5},{7,6},{8,11},{9,8},{10,9... | collective-permute-start | bytes 589832 | tf_op jit(solution)/shard_map/ppermute | solution.py:37
  446.5 7.8 %collective-permute-start.25 = (bf16[128,384]{1,0:T(8,128)(2,1)S(1)}, bf16[128,384]{1,0:T(8,128)(2,1)S(1)}, u32[]{:S(2)}, u32[]{:S(2)}) collective-permute-start(bf16[128,384]{1,0:T(8,128)(2,1)S(1)} %get-tuple-element.60), channel_id=1, source_target_pairs={{0,64},{64,0},{1,65},{65,1},{2,66},{66,2},{3,67},{67,3},{4,68},{68... | collective-permute-start | bytes 294920 | tf_op jit(solution)/shard_map/ppermute | solution.py:18
